TPU v7x, 256 devices: a whole 4x4x8 slice. The times are simulated.
256 devices in a mesh: gx: 8 (over z), gy: 4 (over y_hi, core), gz: 8 (over x, y_lo).
Axes of the slice: x: 4, y: 4 (y_hi: 2, y_lo: 2; y = y_hi * 2 + y_lo), z: 8, core: 2. Of those that a mesh axis runs over, the one named last changes fastest.
Arguments:
- tokens: bfloat16 [1536, 8192], P(('gx', 'gy'), 'gz'), may hold values from -6 to 6
- cotangent: bfloat16 [1536, 8192], P(('gx', 'gy'), 'gz'), may hold values from -6 to 6
- gate_weight: bfloat16 [8192, 14336], P('gz', ('gx', 'gy')), may hold values from -0.0625 to 0.0625
- up_weight: bfloat16 [8192, 14336], P('gz', ('gx', 'gy')), may hold values from -0.0625 to 0.0625
- down_weight: bfloat16 [14336, 8192], P(('gx', 'gy'), 'gz'), may hold values from -0.046875 to 0.046875
Outputs:
- input_grad: bfloat16 [1536, 8192], P(('gx', 'gy'), 'gz')
- gate_grad: bfloat16 [8192, 14336], P('gz', ('gx', 'gy'))
- up_grad: bfloat16 [8192, 14336], P('gz', ('gx', 'gy'))
- down_grad: bfloat16 [14336, 8192], P(('gx', 'gy'), 'gz')
All inputs are finite; a program needn't handle non-finite values.
Results may differ from a plain program's by a relative error of at most 0.0055.
Values may be sent and summed in bfloat16 or wider, within the bound.
A program may use at most 128 MiB of HBM per device.

v0:
```python
import jax
import jax.numpy as jnp
from jax import lax
from jax.sharding import PartitionSpec as P


def contract_first(left, right):
    return lax.dot_general(
        left, right, (((0,), (0,)), ((), ())), preferred_element_type=jnp.float32
    )


def contract_last(left, right):
    return lax.dot_general(
        left, right, (((1,), (1,)), ((), ())), preferred_element_type=jnp.float32
    )


def backward_parts(hidden_grad, gate, up, sigmoid_gate):
    up_part = (hidden_grad * gate * sigmoid_gate).astype(jnp.bfloat16)
    gate_part = (hidden_grad * up * sigmoid_gate * (1.0 + gate * (1.0 - sigmoid_gate))).astype(
        jnp.bfloat16
    )
    return (gate_part, up_part)


def on_device(tokens, cotangent, gate_weight, up_weight, down_weight):
    gate_full, up_full, down_full = (gate_weight, up_weight, down_weight)
    token_block, cotangent_block = (
        lax.all_gather(tokens, "gx", axis=0, tiled=True),
        lax.all_gather(cotangent, "gx", axis=0, tiled=True),
    )
    gate_full, up_full, down_full = (
        lax.all_gather(gate_weight, "gy", axis=1, tiled=True),
        lax.all_gather(up_weight, "gy", axis=1, tiled=True),
        lax.all_gather(down_weight, "gy", axis=0, tiled=True),
    )
    gate_term = jnp.dot(token_block, gate_full, preferred_element_type=jnp.float32)
    up_term = jnp.dot(token_block, up_full, preferred_element_type=jnp.float32)
    gate, up = lax.psum((gate_term, up_term), "gz")
    sigmoid_gate = jax.nn.sigmoid(gate)
    hidden = (gate * sigmoid_gate * up).astype(jnp.bfloat16)
    grad_term = contract_last(cotangent_block, down_full)
    hidden_grad = lax.psum(grad_term, "gz")
    gate_part, up_part = backward_parts(hidden_grad, gate, up, sigmoid_gate)
    down_term = contract_first(hidden, cotangent_block)
    gate_wterm = contract_first(token_block, gate_part)
    up_wterm = contract_first(token_block, up_part)
    gate_grad, up_grad, down_grad = (
        lax.psum_scatter(gate_wterm, "gy", scatter_dimension=1, tiled=True),
        lax.psum_scatter(up_wterm, "gy", scatter_dimension=1, tiled=True),
        lax.psum_scatter(down_term, "gy", scatter_dimension=0, tiled=True),
    )
    input_grad = lax.psum_scatter(
        contract_last(gate_part, gate_full) + contract_last(up_part, up_full),
        "gx",
        scatter_dimension=0,
        tiled=True,
    ).astype(jnp.bfloat16)
    return (
        input_grad,
        gate_grad.astype(jnp.bfloat16),
        up_grad.astype(jnp.bfloat16),
        down_grad.astype(jnp.bfloat16),
    )


def solution(mesh):
    return jax.shard_map(
        on_device,
        mesh=mesh,
        in_specs=(
            P(("gx", "gy"), "gz"),
            P(("gx", "gy"), "gz"),
            P("gz", ("gx", "gy")),
            P("gz", ("gx", "gy")),
            P(("gx", "gy"), "gz"),
        ),
        out_specs=(
            P(("gx", "gy"), "gz"),
            P("gz", ("gx", "gy")),
            P("gz", ("gx", "gy")),
            P(("gx", "gy"), "gz"),
        ),
        check_vma=False,
    )
```

profile of v0, /device:TPU:32, one launch (start us, length us, event | category | flops | bytes accessed | tf_op | source)
XLA Modules:
  0.0 779.2 jit_solution(13767291574339985073)
XLA Ops:
  7.2 0.0 copy-start.1
  7.2 0.0 copy-start.2
  7.2 0.0 all-gather.8.cloned.1.call-start
  7.2 0.7 all-gather.8.cloned.1.call-update
  7.9 0.0 all-gather.6.cloned.1.call-start
  8.0 0.7 all-gather.6.cloned.1.call-update
  8.7 0.0 all-gather.4.cloned.1.call-start
  8.7 0.7 all-gather.4.cloned.1.call-update
  9.4 0.0 all-reduce.3.cloned.1.call-start
  9.4 0.0 copy-done.1
  9.5 29.0 %all_gather.17 = bf16[384,1024]{1,0:T(8,128)(2,1)S(1)} all-gather(bf16[48,1024]{1,0:T(8,128)(2,1)S(1)} %copy-done.1), channel_id=1, replica_groups=mesh['gx'=8,'gy'=4,'gz'=8] {'gx'}, dimensions={0}, use_global_device_ids=true | all-gather | bytes 884736 | tf_op jit(solution)/shard_map/all_gather | solution.py:30
  38.5 0.0 copy-done.2
  38.5 26.3 %all_gather.15 = bf16[384,1024]{1,0:T(8,128)(2,1)S(1)} all-gather(bf16[48,1024]{1,0:T(8,128)(2,1)S(1)} %copy-done.2), channel_id=1, replica_groups=mesh['gx'=8,'gy'=4,'gz'=8] {'gx'}, dimensions={0}, use_global_device_ids=true | all-gather | bytes 884736 | tf_op jit(solution)/shard_map/all_gather | solution.py:31
  64.8 0.0 copy-start
  64.8 0.0 all-gather.8.cloned.1.call-done
  64.8 6.0 fusion.5
  70.8 19.2 %all-gather.6.cloned.1.call-done = bf16[1024,1792]{0,1:T(8,128)(2,1)} async-done(((bf16[1024,448]{0,1:T(8,128)(2,1)}), bf16[1024,1792]{0,1:T(8,128)(2,1)}) %all-gather.6.cloned.1.call-update) | async-done | bytes 3670032 | tf_op jit(solution)/shard_map/all_gather | solution.py:35
  90.0 5.2 fusion.4
  95.2 34.2 %all-gather.4.cloned.1.call-done = bf16[1792,1024]{1,0:T(8,128)(2,1)} async-done(((bf16[448,1024]{1,0:T(8,128)(2,1)}), bf16[1792,1024]{1,0:T(8,128)(2,1)}) %all-gather.4.cloned.1.call-update) | async-done | bytes 3670032 | tf_op jit(solution)/shard_map/all_gather | solution.py:36
  129.4 0.0 copy-done
  129.4 5.2 fusion.3
  134.6 0.0 all-reduce.3.cloned.1.call-update
  134.6 0.0 reduce-scatter.5.cloned.1.call-start
  134.7 340.7 %all-reduce.3.cloned.1.call-done = (f32[384,1792]{1,0:T(8,128)}, f32[384,1792]{1,0:T(8,128)}, f32[384,1792]{1,0:T(8,128)}) async-done(((f32[384,1792]{1,0:T(8,128)}, f32[384,1792]{1,0:T(8,128)}, f32[384,1792]{1,0:T(8,128)}), (f32[384,1792]{1,0:T(8,128)}, f32[384,1792]{1,0:T(8,128)}, f32[384,1792]{1,0:T(8,128)})) %all-reduce.3.cloned.1.call-update) | async-done | bytes 8257552 | tf_op jit(solution)/shard_map/psum | solution.py:40
  475.4 0.0 copy-start.3
  475.4 4.9 multiply_convert_fusion.1
  480.3 0.0 copy-done.3
  480.3 0.0 copy-start.4
  480.3 1.6 fusion.6
  481.9 0.4 copy-done.4
  482.3 2.8 convolution_add_fusion
  485.1 0.0 reduce-scatter.5.cloned.1.call-update
  485.1 0.0 reduce-scatter.11.cloned.1.call-start
  485.2 7.9 %fusion = f32[1792,1024]{1,0:T(8,128)} fusion(bf16[384,1024]{1,0:T(8,128)(2,1)} %copy-done, f32[384,1792]{1,0:T(8,128)} %get-tuple-element.6, f32[384,1792]{1,0:T(8,128)} %get-tuple-element.4), kind=kOutput, calls=%fused_computation.7 | convolution fusion | flops 1413414912 | bytes 13631488 | tf_op jit(solution)/shard_map/dot_general | solution.py:8
  493.0 0.0 reduce-scatter.11.cloned.1.call-update
  493.1 0.2 reduce-scatter.9.cloned.1.call-start
  493.3 5.0 convolution_bitcast_fusion
  498.3 0.0 reduce-scatter.9.cloned.1.call-update
  498.4 0.0 reduce-scatter.7.cloned.1.call-start
  498.4 5.1 convolution_bitcast_fusion.1
  503.5 0.0 reduce-scatter.7.cloned.1.call-update
  503.5 26.7 %reduce-scatter.5.cloned.1.call-done = f32[48,1024]{1,0:T(8,128)} async-done(((f32[384,1024]{1,0:T(8,128)}), f32[48,1024]{1,0:T(8,128)}) %reduce-scatter.5.cloned.1.call-update) | async-done | bytes 196624 | tf_op jit(solution)/shard_map/reduce_scatter | solution.py:54
  530.2 1.6 convert_element_type.23
  531.8 78.2 %reduce-scatter.11.cloned.1.call-done = f32[448,1024]{1,0:T(8,128)} async-done(((f32[1792,1024]{1,0:T(8,128)}), f32[448,1024]{1,0:T(8,128)}) %reduce-scatter.11.cloned.1.call-update) | async-done | bytes 1835024 | tf_op jit(solution)/shard_map/reduce_scatter | solution.py:52
  610.0 2.6 convert_element_type.27
  612.5 77.2 %reduce-scatter.9.cloned.1.call-done = f32[1024,448]{0,1:T(8,128)} async-done(((f32[1024,1792]{0,1:T(8,128)}), f32[1024,448]{0,1:T(8,128)}) %reduce-scatter.9.cloned.1.call-update) | async-done | bytes 1835024 | tf_op jit(solution)/shard_map/reduce_scatter | solution.py:51
  689.8 2.6 convert_element_type.25
  692.3 77.5 %reduce-scatter.7.cloned.1.call-done = f32[1024,448]{0,1:T(8,128)} async-done(((f32[1024,1792]{0,1:T(8,128)}), f32[1024,448]{0,1:T(8,128)}) %reduce-scatter.7.cloned.1.call-update) | async-done | bytes 1835024 | tf_op jit(solution)/shard_map/reduce_scatter | solution.py:50
  769.8 2.6 convert_element_type.24
Async XLA Ops:
  7.2 2.3 copy-start.1
  7.2 31.3 %copy-start.2 = (bf16[48,1024]{1,0:T(8,128)(2,1)S(1)}, bf16[48,1024]{1,0:T(8,128)(2,1)}, u32[]{:S(2)}) copy-start(bf16[48,1024]{1,0:T(8,128)(2,1)} %param.6) | copy-start | bytes 294916
  7.2 57.6 %all-gather.8.cloned.1.call-start = ((), (), s32[]{:S(2)}) async-start(), calls=%async_computation.6 | async-start | bytes 4587520 | tf_op jit(solution)/shard_map/all_gather | solution.py:34
  7.9 82.1 %all-gather.6.cloned.1.call-start = ((), (), s32[]{:S(2)}) async-start(), calls=%async_computation.5 | async-start | bytes 4587520 | tf_op jit(solution)/shard_map/all_gather | solution.py:35
  8.7 120.7 %all-gather.4.cloned.1.call-start = ((), (), s32[]{:S(2)}) async-start(), calls=%async_computation.4 | async-start | bytes 4587520 | tf_op jit(solution)/shard_map/all_gather | solution.py:36
  9.4 466.0 %all-reduce.3.cloned.1.call-start = ((), (), s32[]{:S(2)}) async-start(), calls=%async_computation.11 | async-start | bytes 16515072 | tf_op jit(solution)/shard_map/psum | solution.py:40
  64.8 64.6 %copy-start = (bf16[384,1024]{1,0:T(8,128)(2,1)}, bf16[384,1024]{1,0:T(8,128)(2,1)S(1)}, u32[]{:S(2)}) copy-start(bf16[384,1024]{1,0:T(8,128)(2,1)S(1)} %all_gather.15) | copy-start | bytes 2359300
  134.6 395.6 %reduce-scatter.5.cloned.1.call-start = ((), (), s32[]{:S(2)}) async-start(), calls=%async_computation.7 | async-start | bytes 1769472 | tf_op jit(solution)/shard_map/reduce_scatter | solution.py:54
  475.4 4.9 copy-start.3
  480.3 2.0 copy-start.4
  485.1 124.9 %reduce-scatter.11.cloned.1.call-start = ((), (), s32[]{:S(2)}) async-start(), calls=%async_computation.10 | async-start | bytes 9175040 | tf_op jit(solution)/shard_map/reduce_scatter | solution.py:52
  493.1 196.7 %reduce-scatter.9.cloned.1.call-start = ((), (), s32[]{:S(2)}) async-start(), calls=%async_computation.9 | async-start | bytes 9175040 | tf_op jit(solution)/shard_map/reduce_scatter | solution.py:51
  498.4 271.5 %reduce-scatter.7.cloned.1.call-start = ((), (), s32[]{:S(2)}) async-start(), calls=%async_computation.8 | async-start | bytes 9175040 | tf_op jit(solution)/shard_map/reduce_scatter | solution.py:50
Sparse Core Ops, SparseCore 0:
  9.8 40.7 all-gather.7
  52.4 37.5 all-gather.5
  91.8 37.5 all-gather.3
  134.8 340.5 all-reduce.2
  485.2 44.9 reduce-scatter.4
  533.1 76.8 reduce-scatter.10
  612.8 76.9 reduce-scatter.8
  692.8 76.9 reduce-scatter.6
where the time goes:
time: 781 us; the launch traced here: 779 us
  waiting for transfers between devices  656 us (84%)
  blocking collectives  55.4 us (7%)
  matrix products  38.8 us (5%)
  between operations  14.2 us (2%)
  other arithmetic  14.1 us (2%)
    psum x1, waiting for transfers between devices, on_device(): gate, up = lax.psum((gate_term, up_term), 'gz')  341 us
    reduce_scatter x1, waiting for transfers between devices, on_device(): lax.psum_scatter(down_term, 'gy', scatter_dimension=0, tiled=True)  78.2 us
    reduce_scatter x1, waiting for transfers between devices, on_device(): lax.psum_scatter(gate_wterm, 'gy', scatter_dimension=1, tiled=True)  77.5 us
    reduce_scatter x1, waiting for transfers between devices, on_device(): lax.psum_scatter(up_wterm, 'gy', scatter_dimension=1, tiled=True)  77.2 us
    all_gather x1, waiting for transfers between devices, on_device(): lax.all_gather(down_weight, 'gy', axis=0, tiled=True)  34.2 us
    all_gather x1, blocking collectives, on_device(): lax.all_gather(tokens, 'gx', axis=0, tiled=True)  29 us
    reduce_scatter x1, waiting for transfers between devices, on_device(): lax.psum_scatter(contract_last(gate_part, gate_full) + contract_last(up_p...  26.7 us
    all_gather x1, blocking collectives, on_device(): lax.all_gather(cotangent, 'gx', axis=0, tiled=True)  26.3 us
  transfers between devices with their start and end apart: 8, of which 7 were waited for; matrix products, arithmetic and copies ran while one was open for 5% of the time, Pallas kernels for 0%

commit v1 on v0

v1 whole, which is shorter than its diff:
```python
import jax
import jax.numpy as jnp
from jax import lax
from jax.sharding import PartitionSpec as P

BLOCKS = ("gx", "gy")


def contract(left, right, dims):
    return lax.dot_general(left, right, ((dims[:1], dims[1:]), ((), ())), preferred_element_type=jnp.float32)


def summed(terms, axes, parts):
    rows, columns = terms.shape
    sent = terms.astype(jnp.bfloat16).reshape(parts, rows // parts, columns)
    landed = lax.all_to_all(sent, axes, split_axis=0, concat_axis=0)
    return jnp.sum(landed.astype(jnp.float32), axis=0)


def solution(mesh):
    depth = mesh.shape["gz"]
    blocks = mesh.shape["gx"] * mesh.shape["gy"]

    def on_device(tokens, cotangent, gate_weight, up_weight, down_weight):
        tokens_all = lax.all_gather(tokens, BLOCKS, axis=0, tiled=True)
        cotangent_all = lax.all_gather(cotangent, BLOCKS, axis=0, tiled=True)
        hidden_units = gate_weight.shape[1]
        terms = jnp.concatenate(
            [
                contract(tokens_all, gate_weight, (1, 0)).astype(jnp.bfloat16),
                contract(tokens_all, up_weight, (1, 0)).astype(jnp.bfloat16),
                contract(cotangent_all, down_weight, (1, 1)).astype(jnp.bfloat16),
            ],
            axis=1,
        )
        sums = summed(terms, "gz", depth)
        gate, up, hidden_grad = jnp.split(sums, [hidden_units, 2 * hidden_units], axis=1)
        sigmoid_gate = jax.nn.sigmoid(gate)
        hidden = gate * sigmoid_gate * up
        up_part = hidden_grad * gate * sigmoid_gate
        gate_part = hidden_grad * up * sigmoid_gate * (1.0 + gate * (1.0 - sigmoid_gate))
        parts = jnp.concatenate([hidden, up_part, gate_part], axis=1).astype(jnp.bfloat16)
        parts = lax.all_gather(parts, "gz", axis=0, tiled=True)
        hidden, up_part, gate_part = jnp.split(parts, [hidden_units, 2 * hidden_units], axis=1)
        input_term = contract(gate_part, gate_weight, (1, 1)) + contract(up_part, up_weight, (1, 1))
        input_grad = summed(input_term, BLOCKS, blocks).astype(jnp.bfloat16)
        gate_grad = contract(tokens_all, gate_part, (0, 0)).astype(jnp.bfloat16)
        up_grad = contract(tokens_all, up_part, (0, 0)).astype(jnp.bfloat16)
        down_grad = contract(hidden, cotangent_all, (0, 0)).astype(jnp.bfloat16)
        return input_grad, gate_grad, up_grad, down_grad

    by_row, by_column = P(BLOCKS, "gz"), P("gz", BLOCKS)
    return jax.shard_map(
        on_device,
        mesh=mesh,
        in_specs=(by_row, by_row, by_column, by_column, by_row),
        out_specs=(by_row, by_column, by_column, by_row),
        check_vma=False,
    )
```

time: 781 us -> 443 us (0.57)
  waiting for transfers between devices: 656 us -> 319 us
  matrix products: 38.8 us -> 28.9 us
  starting transfers between devices: 0.5 us -> 10.1 us
    psum x1 -> x0, waiting for transfers between devices: 341 us -> none  [on_device(): gate, up = lax.psum((gate_term, up_term), 'gz')]
    reduce_scatter x4 -> x0, waiting for transfers between devices: 260 us -> none  [the longest x1 78.2 us: on_device(): lax.psum_scatter(down_term, 'gy', scatter_dimension=0, tiled=True)]
    all_gather x3, waiting for transfers between devices: 53.4 us -> 255 us  [the longest x1 91.5 us: on_device(): parts = lax.all_gather(parts, 'gz', axis=0, tiled=True)]
    all_to_all x0 -> x1, waiting for transfers between devices: none -> 62.7 us  [summed(): landed = lax.all_to_all(sent, axes, split_axis=0, concat_axis=0)]
    all_gather x2 -> x0, blocking collectives: 55.4 us -> none  [the longest x1 29 us: on_device(): lax.all_gather(tokens, 'gx', axis=0, tiled=True)]
    all_to_all x0 -> x1, blocking collectives: none -> 55.3 us  [summed(): landed = lax.all_to_all(sent, axes, split_axis=0, concat_axis=0)]
    convert_element_type x5 -> x0, other arithmetic: 14.1 us -> none  [the longest x1 4.88 us: backward_parts(): up_part = (hidden_grad * gate * sigmoid_gate).astype(jnp.bfloat16)]
    all_to_all x0 -> x1, starting transfers between devices: none -> 10 us  [summed(): landed = lax.all_to_all(sent, axes, split_axis=0, concat_axis=0)]
  transfers between devices with their start and end apart: 8 -> 4, of which waited for: 7 -> 4; matrix products, arithmetic and copies ran while one was open for 5% -> 4% of each run, Pallas kernels for 0% -> 0%
where the time goes in v1:
time: 443 us; the launch traced here: 441 us
  waiting for transfers between devices  319 us (72%)
  blocking collectives  55.3 us (12%)
  matrix products  28.9 us (7%)
  between operations  13.9 us (3%)
  starting transfers between devices  10.1 us (2%)
  local copies, waits for them, and re-layouts  7.58 us (2%)
  other arithmetic  6.38 us (1%)
    all_gather x1, waiting for transfers between devices, on_device(): parts = lax.all_gather(parts, 'gz', axis=0, tiled=True)  91.5 us
    all_gather x1, waiting for transfers between devices, on_device(): tokens_all = lax.all_gather(tokens, BLOCKS, axis=0, tiled=True)  87.5 us
    all_gather x1, waiting for transfers between devices, on_device(): cotangent_all = lax.all_gather(cotangent, BLOCKS, axis=0, tiled=True)  76.2 us
    all_to_all x1, waiting for transfers between devices, summed(): landed = lax.all_to_all(sent, axes, split_axis=0, concat_axis=0)  62.7 us
    all_to_all x1, blocking collectives, summed(): landed = lax.all_to_all(sent, axes, split_axis=0, concat_axis=0)  55.3 us
    dot_general x8, matrix products, contract(): lax.dot_general(left, right, ((dims[:1], dims[1:]), ((), ())), preferred_...  28.9 us
    all_to_all x1, starting transfers between devices, summed(): landed = lax.all_to_all(sent, axes, split_axis=0, concat_axis=0)  10 us
  transfers between devices with their start and end apart: 4, of which 4 were waited for; matrix products, arithmetic and copies ran while one was open for 4% of the time, Pallas kernels for 0%

profile of v1, /device:TPU:32, one launch (start us, length us, event | category | flops | bytes accessed | tf_op | source)
XLA Modules:
  0.0 441.5 jit_solution(9989623042914159673)
XLA Ops:
  7.2 0.0 copy-start
  7.2 0.0 all-gather.4.cloned.1.call-start
  7.2 0.7 all-gather.4.cloned.1.call-update
  7.9 0.0 all-gather.6.cloned.1.call-start
  8.0 0.7 all-gather.6.cloned.1.call-update
  8.7 0.0 all-gather.8.cloned.1.call-start
  8.7 87.5 %all-gather.4.cloned.1.call-done = bf16[1536,1024]{1,0:T(8,128)(2,1)} async-done(((bf16[48,1024]{1,0:T(8,128)(2,1)}), bf16[1536,1024]{1,0:T(8,128)(2,1)}) %all-gather.4.cloned.1.call-update) | async-done | bytes 3145744 | tf_op jit(solution)/shard_map/all_gather | solution.py:25
  96.3 0.0 copy-start.3
  96.3 3.9 convolution_convert_fusion.1
  100.2 0.0 copy-done
  100.2 0.0 copy-done.3
  100.2 0.0 copy-start.5
  100.2 2.7 convolution_convert_fusion.2
  102.9 76.2 %all-gather.6.cloned.1.call-done = bf16[1536,1024]{1,0:T(8,128)(2,1)} async-done(((bf16[48,1024]{1,0:T(8,128)(2,1)}), bf16[1536,1024]{1,0:T(8,128)(2,1)}) %all-gather.6.cloned.1.call-update) | async-done | bytes 3145744 | tf_op jit(solution)/shard_map/all_gather | solution.py:26
  179.1 0.0 copy-done.5
  179.1 0.0 copy-start.1
  179.1 3.6 convolution_convert_fusion
  182.7 0.0 copy-done.1
  182.7 2.3 pad_maximum_fusion
  185.0 6.5 %copy.9 = bf16[1536,1344]{1,0:T(8,128)(2,1)} copy(bf16[1536,1344]{0,1:T(8,128)(2,1)} %pad_maximum_fusion) | data formatting | bytes 8257536 | tf_op jit(solution)/shard_map/concatenate | solution.py:28
  191.5 55.3 %all_to_all.10 = bf16[8,192,1344]{2,1,0:T(8,128)(2,1)S(1)} all-to-all(bf16[8,192,1344]{2,1,0:T(8,128)(2,1)} %bitcast.17), channel_id=1, replica_groups=mesh['gx'=8,'gy'=4,'gz'=8] {'gz'}, dimensions={0} | all-to-all | bytes 8257536 | tf_op jit(solution)/shard_map/all_to_all | solution.py:16
  246.8 0.6 convert_reduce_fusion
  247.5 0.3 multiply_convert_fusion
  247.8 1.0 concatenate.8
  248.8 0.0 all-gather.8.cloned.1.call-update
  248.8 0.0 copy-start.2
  248.9 91.5 %all-gather.8.cloned.1.call-done = bf16[1536,1344]{1,0:T(8,128)(2,1)} async-done(((bf16[192,1344]{1,0:T(8,128)(2,1)}), bf16[1536,1344]{1,0:T(8,128)(2,1)}) %all-gather.8.cloned.1.call-update) | async-done | bytes 4128784 | tf_op jit(solution)/shard_map/all_gather | solution.py:43
  340.3 3.2 fusion.8
  343.5 0.0 copy-done.2
  343.5 5.2 %add_convert_fusion = bf16[1536,1024]{1,0:T(8,128)(2,1)} fusion(f32[1536,1024]{1,0:T(8,128)S(1)} %fusion.8, bf16[1024,448]{0,1:T(8,128)(2,1)S(1)} %copy-done.2, bf16[1536,1344]{1,0:T(8,128)(2,1)} %all-gather.8.cloned.1.call-done), kind=kOutput, calls=%fused_computation.1 | convolution fusion | flops 1412431872 | bytes 11927552 | tf_op jit(solution)/shard_map/dot_general | solution.py:10
  348.7 0.0 slice-start
  348.7 10.0 %all-to-all-start.1 = ((bf16[32,48,1024]{2,1,0:T(8,128)(2,1)}), bf16[32,48,1024]{2,1,0:T(8,128)(2,1)}, u32[]{:S(2)}, u32[]{:S(2)}) async-start(bf16[32,48,1024]{2,1,0:T(8,128)(2,1)} %bitcast.18), calls=%async_computation.1 | async-start | bytes 6291456 | tf_op jit(solution)/shard_map/all_to_all | solution.py:16
  358.7 0.0 slice-start.1
  358.8 0.0 copy-start.4
  358.8 5.1 %fusion.2 = bf16[448,1024]{1,0:T(8,128)(2,1)} fusion(bf16[1536,1024]{1,0:T(8,128)(2,1)} %all-gather.6.cloned.1.call-done, bf16[1536,1344]{1,0:T(8,128)(2,1)} %all-gather.8.cloned.1.call-done), kind=kOutput, calls=%fused_computation.8 | convolution fusion | flops 1409744896 | bytes 5636096 | tf_op jit(solution)/shard_map/dot_general | solution.py:10
  363.8 0.0 slice-done
  363.8 0.0 slice-done.1
  363.8 0.0 copy-done.4
  363.8 2.6 fusion.10
  366.4 2.7 fusion.13
  369.1 62.7 %all-to-all-done.1 = bf16[32,48,1024]{2,1,0:T(8,128)(2,1)} async-done(((bf16[32,48,1024]{2,1,0:T(8,128)(2,1)}), bf16[32,48,1024]{2,1,0:T(8,128)(2,1)}, u32[]{:S(2)}, u32[]{:S(2)}) %all-to-all-start.1) | async-done | bytes 3145760 | tf_op jit(solution)/shard_map/all_to_all | solution.py:16
  431.8 3.2 reduce_sum.22
  (1 shorter events, 0.0 us)
Async XLA Ops:
  7.2 93.0 %copy-start = (bf16[1024,448]{0,1:T(8,128)(2,1)S(1)}, bf16[1024,448]{0,1:T(8,128)(2,1)}, u32[]{:S(2)}) copy-start(bf16[1024,448]{0,1:T(8,128)(2,1)} %param.7) | copy-start | bytes 2752516
  7.2 89.1 %all-gather.4.cloned.1.call-start = ((), (), s32[]{:S(2)}) async-start(), calls=%async_computation.2 | async-start | bytes 3244032 | tf_op jit(solution)/shard_map/all_gather | solution.py:25
  7.9 171.2 %all-gather.6.cloned.1.call-start = ((), (), s32[]{:S(2)}) async-start(), calls=%async_computation.3 | async-start | bytes 3244032 | tf_op jit(solution)/shard_map/all_gather | solution.py:26
  8.7 331.7 %all-gather.8.cloned.1.call-start = ((), (), s32[]{:S(2)}) async-start(), calls=%async_computation.4 | async-start | bytes 4866048 | tf_op jit(solution)/shard_map/all_gather | solution.py:43
  96.3 3.9 copy-start.3
  100.2 78.9 %copy-start.5 = (bf16[448,1024]{1,0:T(8,128)(2,1)S(1)}, bf16[448,1024]{1,0:T(8,128)(2,1)}, u32[]{:S(2)}) copy-start(bf16[448,1024]{1,0:T(8,128)(2,1)} %param.9) | copy-start | bytes 2752516
  179.1 3.6 copy-start.1
  248.8 94.7 %copy-start.2 = (bf16[1024,448]{0,1:T(8,128)(2,1)S(1)}, bf16[1024,448]{0,1:T(8,128)(2,1)}, u32[]{:S(2)}) copy-start(bf16[1024,448]{0,1:T(8,128)(2,1)} %param.8) | copy-start | bytes 2752516
  348.7 15.1 %slice-start = ((s8[4325376]{0:T(1024)(128)(4,1)}), s8[131072]{0:T(1024)(128)(4,1)S(1)}, s32[]{:S(2)}) async-start(s8[4325376]{0:T(1024)(128)(4,1)} %bitcast.19), calls=%async_computation.5 | async-start | bytes 262144
  348.7 83.1 %all-to-all-start.1 = ((bf16[32,48,1024]{2,1,0:T(8,128)(2,1)}), bf16[32,48,1024]{2,1,0:T(8,128)(2,1)}, u32[]{:S(2)}, u32[]{:S(2)}) async-start(bf16[32,48,1024]{2,1,0:T(8,128)(2,1)} %bitcast.18), calls=%async_computation.1 | async-start | bytes 6291456 | tf_op jit(solution)/shard_map/all_to_all | solution.py:16
  358.7 5.1 %slice-start.1 = ((s8[4325376]{0:T(1024)(128)(4,1)}), s8[4194304]{0:T(1024)(128)(4,1)S(1)}, s32[]{:S(2)}) async-start(s8[4325376]{0:T(1024)(128)(4,1)} %bitcast.19), calls=%async_computation.6 | async-start | bytes 8388608
  358.8 5.1 %copy-start.4 = (bf16[1536,1024]{1,0:T(8,128)(2,1)S(1)}, bf16[1536,1024]{1,0:T(8,128)(2,1)}, u32[]{:S(2)}) copy-start(bf16[1536,1024]{1,0:T(8,128)(2,1)} %all-gather.4.cloned.1.call-done) | copy-start | bytes 9437188
Sparse Core Ops, SparseCore 0:
  10.8 85.4 all-gather.3
  99.0 80.0 all-gather.5
  249.0 91.3 all-gather.7

commit v2 on v1

v2 whole, which is shorter than its diff:
```python
import functools

import jax
import jax.numpy as jnp
from jax import lax
from jax.experimental import pallas as pl
from jax.experimental.pallas import tpu as pltpu
from jax.sharding import PartitionSpec as P

F32, BF16 = jnp.float32, jnp.bfloat16
SLOTS = (0, 1, -1, 2, -2, 3, -3, 4)
CHUNKS = (128, 384, 384, 384, 256)
OFFSETS = tuple(sum(CHUNKS[:i]) for i in range(len(CHUNKS)))
COPIES = 224


def dot_nn(a, b):
    return lax.dot_general(a, b, (((1,), (0,)), ((), ())), preferred_element_type=F32)


def dot_nt(a, b):
    return lax.dot_general(a, b, (((1,), (1,)), ((), ())), preferred_element_type=F32)


def dot_tn(a, b):
    return lax.dot_general(a, b, (((0,), (0,)), ((), ())), preferred_element_type=F32)


def kernel(
    tok_in, cot_in, gw_in, uw_in, dw_in,
    ig_out, gg_out, ug_out, dg_out,
    act, gw, uw, wgu, dw,
    gu_s1, gu_r1, gu_own, gu_s2, gu_r2,
    h_s1, h_own, h_r1, h_s2, h_r2, h_fin,
    pa, pb, ip, d_r1, d_s2, d_r2, d_s3, d_r3,
    acc_gu, acc_d, gg_v, ug_v, dg_v, ig_v,
    send_sem, recv_sem, local_sem,
):
    rows, units = tok_in.shape[0], gw_in.shape[1]
    z, gy, gz = lax.axis_index("gx"), lax.axis_index("gy"), lax.axis_index("gz")
    yh, core, x, yl = gy // 2, gy % 2, gz // 2, gz % 2
    sibling = (z, yh * 2 + (1 - core), gz)
    far = (z, (1 - yh) * 2 + core, gz)
    near = (z, gy, x * 2 + (1 - yl))

    def along_z(d):
        return (lax.rem(z + 8 + d, 8), gy, gz)

    def x_of(d):
        return lax.rem(x + d, 4)

    def along_x(d):
        return (z, gy, x_of(d) * 2 + yl)

    def at(start, n):
        return pl.ds(pl.multiple_of(start, 16), n)

    copies = []

    def send(src, dst, device):
        i = len(copies)
        copy = pltpu.make_async_remote_copy(
            src_ref=src, dst_ref=dst, send_sem=send_sem.at[i], recv_sem=recv_sem.at[i],
            device_id=device, device_id_type=pl.DeviceIdType.MESH,
        )
        copy.start()
        copies.append(copy)
        return copy

    locals_ = []

    def local(src, dst):
        copy = pltpu.make_async_copy(src, dst, local_sem.at[len(locals_)])
        copy.start()
        locals_.append(copy)
        return copy

    own = [local(tok_in, act.at[0, pl.ds(0, rows)]), local(cot_in, act.at[1, pl.ds(0, rows)])]
    weights = [local(gw_in, gw), local(uw_in, uw), local(dw_in, dw)]

    barrier = pltpu.get_barrier_semaphore()
    peers = [sibling, far, near] + [along_x(d) for d in (1, 2, 3)] + [along_z(d) for d in range(1, 8)]
    for peer in peers:
        pl.semaphore_signal(barrier, inc=1, device_id=peer, device_id_type=pl.DeviceIdType.MESH)
    pl.semaphore_wait(barrier, len(peers))

    got, sib = {}, {}
    slot = {d: s * 4 * rows for s, d in enumerate(SLOTS)}

    def part(d, h, which=None):
        span = pl.ds(slot[d] + h * rows, rows)
        return act.at[:, span] if which is None else act.at[which, span]

    def ring(j, h):
        for sign in (1, -1):
            which = None if j < 4 else (0 if sign == 1 else 1)
            src, dst = -sign * (j - 1), (-sign * j if j < 4 else 4)
            got[sign, j, h] = send(part(src, h, which), part(dst, h, which), along_z(sign))

    def to_sibling(d, which=None):
        a, b = pl.ds(slot[d], 2 * rows), pl.ds(slot[d] + 2 * rows, 2 * rows)
        if which is None:
            return send(act.at[:, a], act.at[:, b], sibling)
        return send(act.at[which, a], act.at[which, b], sibling)

    def start_a():
        for copy in own:
            copy.wait()
        yh_copy = send(part(0, 0), part(0, 1), far)
        ring(1, 0)
        first = send(act.at[:, pl.ds(0, rows)], act.at[:, pl.ds(2 * rows, rows)], sibling)
        yh_copy.wait_recv()
        ring(1, 1)
        second = send(act.at[:, pl.ds(rows, rows)], act.at[:, pl.ds(3 * rows, rows)], sibling)
        for copy in weights:
            copy.wait()
        wgu[...] = jnp.concatenate([gw[...], uw[...]], axis=1)
        first.wait_recv()
        second.wait_recv()

    def forward(j, h):
        for sign in (1, -1):
            got[sign, j, h].wait_recv()
        if j < 4:
            ring(j + 1, h)
        if h == 1:
            if j < 4:
                sib[j] = [to_sibling(j), to_sibling(-j)]
            else:
                sib[j] = [to_sibling(4, 0), to_sibling(4, 1)]

    def siblings(j):
        for copy in sib[j]:
            copy.wait_recv()

    gu1, gu2, h1, h2 = {}, {}, {}, {}

    def s1(k):
        o, n = OFFSETS[k], CHUNKS[k]
        q, r = n // 2, n // 8
        half = pl.ds(o // 2, q)
        gu_s1[half] = dot_nn(act[0, at(o + (1 - yl) * q, q)], wgu[...]).astype(BF16)
        gu1[k] = send(gu_s1.at[half], gu_r1.at[half], near)
        term = dot_nt(act[1, pl.ds(o, n)], dw[...])
        h_own[pl.ds(o, n)] = term
        h_s1[pl.ds(o, n)] = term.astype(BF16)
        h1[k] = [
            send(h_s1.at[at(o + y * q + x_of(d) * r, r)], h_r1.at[d - 1, y, pl.ds(o // 8, r)], along_x(d))
            for d in (1, 3, 2) for y in (0, 1)
        ]
        gu_own[half] = dot_nn(act[0, at(o + yl * q, q)], wgu[...])

    def s2(k):
        o, n = OFFSETS[k], CHUNKS[k]
        q, r = n // 2, n // 8
        half, piece = pl.ds(o // 2, q), pl.ds(o // 8, r)
        gu1[k].wait_recv()
        gu_s2[half] = (gu_own[half] + gu_r1[half].astype(F32)).astype(BF16)
        gu2[k] = [
            send(gu_s2.at[at(o // 2 + x_of(d) * r, r)], gu_r2.at[d - 1, piece], along_x(d)) for d in (1, 3, 2)
        ]
        for copy in h1[k]:
            copy.wait_recv()

        def total(y):
            value = h_own[at(o + y * q + x * r, r)]
            for d in range(3):
                value = value + h_r1[d, y, piece].astype(F32)
            return value

        h_s2[piece] = total(1 - yl).astype(BF16)
        h2[k] = send(h_s2.at[piece], h_r2.at[piece], near)
        h_fin[piece] = total(yl)

    pa_y, pa_x, pb_y, pb_x, pa_xx, pb_yy = {}, {}, {}, {}, {}, {}

    def s3(k):
        o, n = OFFSETS[k], CHUNKS[k]
        q, r = n // 2, n // 8
        piece, mine = pl.ds(o // 8, r), at(o + yl * q + x * r, r)
        for copy in gu2[k]:
            copy.wait_recv()
        h2[k].wait_recv()
        kept = at(o // 2 + x * r, r)
        gu = gu_own[kept] + gu_r1[kept].astype(F32)
        for d in range(3):
            gu = gu + gu_r2[d, piece].astype(F32)
        hidden_grad = h_fin[piece] + h_r2[piece].astype(F32)
        gate, up = gu[:, :units], gu[:, units:]
        sigmoid_gate = jax.nn.sigmoid(gate)
        pb[mine] = (gate * sigmoid_gate * up).astype(BF16)
        up_part = hidden_grad * gate * sigmoid_gate
        gate_part = hidden_grad * up * sigmoid_gate * (1.0 + gate * (1.0 - sigmoid_gate))
        pa[mine] = jnp.concatenate([gate_part, up_part], axis=1).astype(BF16)
        pa_y[k] = send(pa.at[mine], pa.at[mine], near)
        pb_x[k] = [send(pb.at[mine], pb.at[mine], along_x(d)) for d in (1, 3, 2)]
        pa_x[k] = [send(pa.at[mine], pa.at[mine], along_x(d)) for d in (1, 3, 2)]
        pb_y[k] = send(pb.at[mine], pb.at[mine], near)

    def s4(k):
        o, n = OFFSETS[k], CHUNKS[k]
        q, r = n // 2, n // 8
        pa_y[k].wait_recv()
        other = at(o + (1 - yl) * q + x * r, r)
        pa_xx[k] = [send(pa.at[other], pa.at[other], along_x(d)) for d in (1, 3, 2)]
        pb_yy[k] = []
        for copy, d in zip(pb_x[k], (1, 3, 2)):
            copy.wait_recv()
            theirs = at(o + yl * q + x_of(4 - d) * r, r)
            pb_yy[k].append(send(pb.at[theirs], pb.at[theirs], near))

    def s5(k):
        for copy in pa_x[k] + pa_xx[k]:
            copy.wait_recv()
        span = pl.ds(OFFSETS[k], CHUNKS[k])
        ip[span] = dot_nt(pa[span], wgu[...])

    def s6(k):
        span = pl.ds(OFFSETS[k], CHUNKS[k])
        pb_y[k].wait_recv()
        for copy in pb_yy[k]:
            copy.wait_recv()
        gu_term = dot_tn(act[0, span], pa[span])
        acc_gu[...] = gu_term if k == 0 else acc_gu[...] + gu_term
        d_term = dot_tn(pb[span], act[1, span])
        acc_d[...] = d_term if k == 0 else acc_d[...] + d_term

    dc, dy, dz = {}, {}, {}

    def d1(s):
        dc[s] = send(ip.at[pl.ds((s * 4 + 2) * rows, 2 * rows)], d_r1.at[s], sibling)

    def d2(s):
        dc[s].wait_recv()
        d_s2[s] = (ip[pl.ds((s * 4 + 1) * rows, rows)] + d_r1[s, pl.ds(rows, rows)]).astype(BF16)
        dy[s] = send(d_s2.at[s], d_r2.at[s], far)

    def d3(s):
        dy[s].wait_recv()
        value = ip[pl.ds(s * 4 * rows, rows)] + d_r1[s, pl.ds(0, rows)] + d_r2[s].astype(F32)
        if s == 0:
            ip[pl.ds(0, rows)] = value
        else:
            d_s3[s] = value.astype(BF16)
            dz[s] = send(d_s3.at[s], d_r3.at[s - 1], along_z(SLOTS[s]))

    def d4():
        value = ip[pl.ds(0, rows)]
        for s in range(1, 8):
            dz[s].wait_recv()
            value = value + d_r3[s - 1].astype(F32)
        ig_v[...] = value.astype(BF16)

    start_a()
    s1(0)
    forward(1, 0)
    forward(1, 1)
    siblings(1)
    s1(1)
    s2(0)
    forward(2, 0)
    s3(0)
    forward(2, 1)
    siblings(2)
    s1(2)
    s2(1)
    s4(0)
    forward(3, 0)
    forward(3, 1)
    siblings(3)
    s1(3)
    s3(1)
    s5(0)
    forward(4, 0)
    forward(4, 1)
    s6(0)
    siblings(4)
    s1(4)
    s2(2)
    s4(1)
    s3(2)
    s5(1)
    d1(0)
    d1(1)
    s6(1)
    s2(3)
    s4(2)
    s3(3)
    d2(1)
    d2(0)
    s5(2)
    d1(2)
    d1(3)
    s2(4)
    s6(2)
    d3(1)
    d3(0)
    s4(3)
    s3(4)
    d2(2)
    d2(3)
    s5(3)
    d1(4)
    d1(5)
    s4(4)
    d3(2)
    d3(3)
    s6(3)
    d2(4)
    d2(5)
    s5(4)
    d1(7)
    d1(6)
    d3(4)
    d3(5)
    d2(7)
    d2(6)
    s6(4)
    d3(7)
    d3(6)
    gg_v[...] = acc_gu[:, :units].astype(BF16)
    ug_v[...] = acc_gu[:, units:].astype(BF16)
    dg_v[...] = acc_d[...].astype(BF16)
    outs = [local(gg_v, gg_out), local(ug_v, ug_out), local(dg_v, dg_out)]
    d4()
    outs.append(local(ig_v, ig_out))
    for copy in copies:
        copy.wait_send()
    for copy in outs:
        copy.wait()


def on_device(tokens, cotangent, gate_weight, up_weight, down_weight):
    rows, width = tokens.shape
    units = gate_weight.shape[1]
    n = rows * 32
    scratch = [
        ((2, n, width), BF16), ((width, units), BF16), ((width, units), BF16),
        ((width, 2 * units), BF16), ((units, width), BF16),
        ((n // 2, 2 * units), BF16), ((n // 2, 2 * units), BF16), ((n // 2, 2 * units), F32),
        ((n // 2, 2 * units), BF16), ((3, n // 8, 2 * units), BF16),
        ((n, units), BF16), ((n, units), F32), ((3, 2, n // 8, units), BF16),
        ((n // 8, units), BF16), ((n // 8, units), BF16), ((n // 8, units), F32),
        ((n, 2 * units), BF16), ((n, units), BF16),
        ((n, width), F32), ((8, 2 * rows, width), F32), ((8, rows, width), BF16),
        ((8, rows, width), BF16), ((8, rows, width), BF16), ((7, rows, width), BF16),
        ((width, 2 * units), F32), ((units, width), F32),
        ((width, units), BF16), ((width, units), BF16), ((units, width), BF16), ((rows, width), BF16),
    ]
    flops = 16 * n * width * units
    return pl.pallas_call(
        kernel,
        out_shape=[
            jax.ShapeDtypeStruct(a.shape, BF16) for a in (tokens, gate_weight, up_weight, down_weight)
        ],
        in_specs=[pl.BlockSpec(memory_space=pl.ANY)] * 5,
        out_specs=[pl.BlockSpec(memory_space=pl.ANY)] * 4,
        scratch_shapes=[pltpu.VMEM(shape, dtype) for shape, dtype in scratch]
        + [
            pltpu.SemaphoreType.DMA((COPIES,)),
            pltpu.SemaphoreType.DMA((COPIES,)),
            pltpu.SemaphoreType.DMA((16,)),
        ],
        compiler_params=pltpu.CompilerParams(
            collective_id=0, has_side_effects=True, vmem_limit_bytes=60 * 2**20
        ),
        cost_estimate=pl.CostEstimate(flops=flops, bytes_accessed=6 * 2**20, transcendentals=n * units // 8),
    )(tokens, cotangent, gate_weight, up_weight, down_weight)


def solution(mesh):
    blocks = ("gx", "gy")
    by_row, by_column = P(blocks, "gz"), P("gz", blocks)
    return jax.shard_map(
        on_device,
        mesh=mesh,
        in_specs=(by_row, by_row, by_column, by_column, by_row),
        out_specs=(by_row, by_column, by_column, by_row),
        check_vma=False,
    )
```

time: 443 us -> 134 us (0.30)
  waiting for transfers between devices: 319 us -> 0 us
  Pallas kernels: 0 us -> 124 us
  blocking collectives: 55.3 us -> 0 us
  matrix products: 28.9 us -> 0 us
  between operations: 13.9 us -> 0.66 us
  starting transfers between devices: 10.1 us -> 0 us
  other arithmetic: 6.38 us -> 0 us
    all_gather x3 -> x0, waiting for transfers between devices: 255 us -> none  [the longest x1 91.5 us: on_device(): parts = lax.all_gather(parts, 'gz', axis=0, tiled=True)]
    pallas_call x0 -> x1, Pallas kernels: none -> 124 us  [on_device(): pl.pallas_call(kernel, out_shape=[jax.ShapeDtypeStruct(a.shape, BF16) for...]
    all_to_all x1 -> x0, waiting for transfers between devices: 62.7 us -> none  [summed(): landed = lax.all_to_all(sent, axes, split_axis=0, concat_axis=0)]
    all_to_all x1 -> x0, blocking collectives: 55.3 us -> none  [summed(): landed = lax.all_to_all(sent, axes, split_axis=0, concat_axis=0)]
    dot_general x8 -> x0, matrix products: 28.9 us -> none  [contract(): lax.dot_general(left, right, ((dims[:1], dims[1:]), ((), ())), preferred_...]
    all_to_all x1 -> x0, starting transfers between devices: 10 us -> none  [summed(): landed = lax.all_to_all(sent, axes, split_axis=0, concat_axis=0)]
    concatenate x2 -> x0, local copies, waits for them, and re-layouts: 7.54 us -> none  [the longest x1 6.5 us: on_device(): jnp.concatenate([contract(tokens_all, gate_weight, (1, 0)).astype(jnp.bfl...]
    unnamed x16 -> x12, local copies, waits for them, and re-layouts: 0.04 us -> 5.2 us
  transfers between devices with their start and end apart: 4 -> 0, of which waited for: 4 -> 0; matrix products, arithmetic and copies ran while one was open for 4% -> 0% of each run, Pallas kernels for 0% -> 0%
where the time goes in v2:
time: 134 us
  Pallas kernels  124 us (93%)
  local copies, waits for them, and re-layouts  8.77 us (7%)
    pallas_call x1, Pallas kernels, on_device(): pl.pallas_call(kernel, out_shape=[jax.ShapeDtypeStruct(a.shape, BF16) for...  124 us
    unnamed x12, local copies, waits for them, and re-layouts  5.2 us
    pallas_call x2, local copies, waits for them, and re-layouts, on_device(): pl.pallas_call(kernel, out_shape=[jax.ShapeDtypeStruct(a.shape, BF16) for...  3.57 us

profile of v2, /device:TPU:32, one launch (start us, length us, event | category | flops | bytes accessed | tf_op | source)
XLA Modules:
  0.0 133.6 jit_solution(17841361089725532329)
XLA Ops:
  0.6 0.0 copy-start.2
  0.6 2.3 %copy.9.gw_in = bf16[1024,448]{1,0:T(8,128)(2,1)} copy(bf16[1024,448]{0,1:T(8,128)(2,1)} %param.7) | data formatting | bytes 1835008 | tf_op args[2]
  3.0 0.0 copy-done.2
  3.0 1.3 copy.10.uw_in
  4.3 124.1 %shard_map.84 = (bf16[48,1024]{1,0:T(8,128)(2,1)}, bf16[1024,448]{1,0:T(8,128)(2,1)}, bf16[1024,448]{1,0:T(8,128)(2,1)}, bf16[448,1024]{1,0:T(8,128)(2,1)}) custom-call(bf16[48,1024]{1,0:T(8,128)(2,1)} %tok_in.1, bf16[48,1024]{1,0:T(8,128)(2,1)} %cot_in.1, bf16[1024,448]{1,0:T(8,128)(2,1)} %copy.9.gw_in, bf16[1024,448]{1,0:T(8,128)(2,1)} %copy.10.uw_in, ...), custom_call_target="tpu_custom_call" | custom-call | flops 11274289152 | bytes 6291456 | tf_op jit(solution)/shard_map/pallas_call | solution.py:351
  128.4 0.0 copy-start
  128.4 2.3 %copy.11 = bf16[1024,448]{0,1:T(8,128)(2,1)} copy(bf16[1024,448]{1,0:T(8,128)(2,1)} %get-tuple-element.5) | data formatting | bytes 1835008 | tf_op jit(solution)/shard_map/pallas_call | solution.py:351
  130.7 0.0 copy-done
  130.7 0.0 copy-start.3
  130.7 0.0 copy-start.1
  130.7 1.3 copy.12
  132.0 0.0 copy-done.3
  132.0 0.6 copy.15
  132.6 0.0 copy-done.1
  132.7 0.9 copy.16
Async XLA Ops:
  0.6 2.3 %copy-start.2 = (bf16[1024,448]{0,1:T(8,128)(2,1)S(1)}, bf16[1024,448]{0,1:T(8,128)(2,1)}, u32[]{:S(2)}) copy-start(bf16[1024,448]{0,1:T(8,128)(2,1)} %param.8) | copy-start | bytes 2752516
  128.4 2.3 %copy-start = (bf16[1024,448]{1,0:T(8,128)(2,1)S(1)}, bf16[1024,448]{1,0:T(8,128)(2,1)}, u32[]{:S(2)}) copy-start(bf16[1024,448]{1,0:T(8,128)(2,1)} %get-tuple-element.6) | copy-start | bytes 2752516
  130.7 1.3 copy-start.3
  130.7 1.9 %copy-start.1 = (bf16[448,1024]{1,0:T(8,128)(2,1)S(1)}, bf16[448,1024]{1,0:T(8,128)(2,1)}, u32[]{:S(2)}) copy-start(bf16[448,1024]{1,0:T(8,128)(2,1)} %get-tuple-element.15) | copy-start | bytes 2752516

commit v3 on v1

v3 whole, which is shorter than its diff:
```python
import jax
import jax.numpy as jnp
from jax import lax
from jax.experimental import pallas as pl
from jax.experimental.pallas import tpu as pltpu
from jax.sharding import PartitionSpec as P

F32, BF16 = jnp.float32, jnp.bfloat16
SLOTS = (0, 1, -1, 2, -2, 3, -3, 4)
UNITS = ((0, 0), (0, 1), (1, 0), (-1, 0), (1, 1), (-1, 1), (2, 0), (-2, 0), (2, 1), (-2, 1), (3, 0), (-3, 0), (3, 1), (-3, 1), (4, 0), (4, 1))
CHUNKS = (128, 128, 128, 128, 128, 128, 128, 128, 128, 128, 128, 128)
X_FIRST = (True, False, False, False, False, True, False, True, False, True, False, False)
FORWARD = (True, False, True, True, True, True, True, True, True, True, True, True)
GROUPS = ((0, 1), (2, 3), (4, 5), (6, 7), (8, 9), (10, 11))
NEAR_Z = (1, -1, 2, -2)
ORDER = (
    ("A0",), ("R", 1, 0), ("A1",), ("s1a", 2), ("s1a", 0), ("s1a", 1), ("s1b", 0), ("s1b", 1), ("s1b", 2),
    ("s2a", 0), ("s2b", 1), ("s2a", 2), ("s2b", 2), ("R", 2, 0), ("s2b", 0), ("s2a", 1), ("R", 1, 1),
    ("s1a", 5), ("s1b", 5), ("s1a", 3), ("s1a", 4), ("s1b", 3), ("s1b", 4), ("s3", 0), ("s3b", 0), ("s3", 2),
    ("s3b", 2), ("s3", 1), ("s3b", 1), ("s2a", 5), ("R", 3, 0), ("s2b", 3), ("s4a", 0), ("R", 2, 1), ("s2b", 4),
    ("s4b", 0), ("s2b", 5), ("s4b", 2), ("s4a", 2), ("s1a", 6), ("s1a", 7), ("s4f1", 0), ("s1b", 6), ("s1b", 7),
    ("s4f1", 2), ("s2a", 3), ("s2a", 4), ("s4a", 1), ("s4b", 1), ("s4c", 0), ("s4f2", 0), ("s4c", 2),
    ("R", 4, 0), ("s3", 5), ("s3b", 5), ("s4f2", 2), ("R", 3, 1), ("s1a", 9), ("s2a", 7), ("s1a", 10),
    ("s2b", 6), ("s1b", 9), ("s1b", 10), ("s4a", 5), ("s2a", 6), ("s1a", 8), ("s1b", 8), ("s2b", 7),
    ("R", 4, 1), ("s3", 3), ("s4b", 5), ("s3b", 3), ("s3", 4), ("s3b", 4), ("s1a", 11), ("s1b", 11), ("s5", 0),
    ("d1", 0, 0), ("s5", 1), ("d1", 0, 1), ("s6", 0), ("s4f1", 5), ("s2a", 9), ("s5", 2), ("d1", 1, 0),
    ("d1", 2, 0), ("s3", 7), ("s3b", 7), ("s2b", 10), ("s4a", 3), ("s2a", 10), ("s2b", 8), ("s4a", 4),
    ("s2b", 9), ("s4c", 5), ("s4b", 3), ("s4b", 4), ("s4f2", 5), ("s2a", 8), ("s2b", 11), ("s3", 6), ("s3b", 6),
    ("s4f1", 3), ("s4a", 7), ("s4f1", 4), ("s2a", 11), ("s4b", 7), ("s3", 9), ("s4f2", 3), ("s3b", 9),
    ("s4f1", 7), ("s4f2", 4), ("s4c", 3), ("s4c", 4), ("s3", 10), ("s3b", 10), ("s4a", 6), ("s5", 5),
    ("d1", 4, 0), ("s4a", 9), ("s4b", 6), ("s4c", 7), ("s4f2", 7), ("s3", 8), ("s3b", 8), ("s4b", 9),
    ("s4a", 10), ("s4f1", 6), ("s5", 3), ("d1", 1, 1), ("s6", 1), ("s4b", 10), ("s4f2", 6), ("d3", 1),
    ("s4f1", 9), ("s3", 11), ("s4f2", 9), ("s4c", 6), ("s3b", 11), ("s4f1", 10), ("s5", 4), ("d1", 2, 1),
    ("d1", 3, 0), ("s5", 7), ("s6", 2), ("s4b", 8), ("s4f2", 10), ("d3", 2), ("s4c", 9), ("s4f1", 8),
    ("s4a", 8), ("s4c", 10), ("s5", 6), ("d1", 3, 1), ("d1", 4, 1), ("s6", 3), ("s4b", 11), ("s4f1", 11),
    ("s4a", 11), ("s5", 9), ("d1", 5, 1), ("d3", 3), ("d3", 4), ("s4c", 8), ("s5", 10), ("d1", 6, 1), ("d2", 5),
    ("s4f2", 8), ("d2", 6), ("s4f2", 11), ("s4c", 11), ("s5", 8), ("d1", 5, 0), ("d1", 6, 0), ("s6", 4),
    ("s5", 11), ("d1", 7, 1), ("d1", 7, 0), ("d3", 5), ("s6", 5), ("d2", 7), ("d3", 6), ("fin",), ("d2", 0),
    ("d3", 7), ("d4",),
)

OFFSETS = tuple(sum(CHUNKS[:i]) for i in range(len(CHUNKS)))
X_ROWS = sum(n for n, m in zip(CHUNKS, X_FIRST) if m)
Y_ROWS = sum(CHUNKS) - X_ROWS
SAME = tuple(
    sum(n for n, m in zip(CHUNKS[:i], X_FIRST) if m == X_FIRST[i]) for i in range(len(CHUNKS))
)
COPIES = 512


def dot(a, b, i, j):
    return lax.dot_general(a, b, (((i,), (j,)), ((), ())), preferred_element_type=F32)


class Sum:
    names = ("own", "s1y", "r1y", "s2x", "r2x", "s1x", "r1x", "s2y", "r2y", "fin")

    def __init__(self, refs):
        for name, ref in zip(self.names, refs):
            setattr(self, name, ref)
        self.first, self.second = {}, {}

    @staticmethod
    def shapes(columns, x_rows, y_rows):
        x, y = max(x_rows, 128), max(y_rows, 128)
        return [
            ((x_rows + y_rows, columns), F32),
            ((y // 2, columns), BF16), ((y // 2, columns), BF16),
            ((y // 2, columns), BF16), ((3, y // 8, columns), BF16),
            ((x, columns), BF16), ((3, 2, x // 8, columns), BF16),
            ((x // 8, columns), BF16), ((x // 8, columns), BF16), ((x // 8, columns), F32),
        ]


def kernel(tok_in, cot_in, gw_in, uw_in, dw_in, ig_out, gg_out, ug_out, dg_out, *scratch):
    act, wgu, dw = scratch[:3]
    gu, h = Sum(scratch[3:13]), Sum(scratch[13:23])
    (
        pa, pb, ip, d_r1, d_s2, d_r2, d_s3, d_r3, d_sz, d_rz,
        acc_gu, acc_d, ig_v, send_sem, recv_sem, local_sem,
    ) = scratch[23:]
    rows, units = tok_in.shape[0], gw_in.shape[0]
    z, gy, gz = lax.axis_index("gx"), lax.axis_index("gy"), lax.axis_index("gz")
    yh, core, x, yl = gy // 2, gy % 2, gz // 2, gz % 2
    sibling = (z, yh * 2 + (1 - core), gz)
    far = (z, (1 - yh) * 2 + core, gz)
    near = (z, gy, x * 2 + (1 - yl))

    def along_z(d):
        return (lax.rem(z + 8 + d, 8), gy, gz)

    def x_of(d):
        return lax.rem(x + d, 4)

    def along_x(d):
        return (z, gy, x_of(d) * 2 + yl)

    def at(start, n):
        return pl.ds(pl.multiple_of(start, 16), n)

    def place(d, half):
        return UNITS.index((d, half)) * 2 * rows

    copies, sent_act = [], []

    def send(src, dst, device):
        i = len(copies)
        copy = pltpu.make_async_remote_copy(
            src_ref=src, dst_ref=dst, send_sem=send_sem.at[i], recv_sem=recv_sem.at[i],
            device_id=device, device_id_type=pl.DeviceIdType.MESH,
        )
        copy.start()
        copies.append(copy)
        return copy

    locals_ = []

    def local(src, dst):
        copy = pltpu.make_async_copy(src, dst, local_sem.at[len(locals_)])
        copy.start()
        locals_.append(copy)
        return copy

    mine = pl.ds(place(0, 0), rows)
    own = [local(tok_in, act.at[0, mine]), local(cot_in, act.at[1, mine])]
    weights = [
        local(gw_in, wgu.at[pl.ds(0, units)]), local(uw_in, wgu.at[pl.ds(units, units)]), local(dw_in, dw)
    ]

    barrier = pltpu.get_barrier_semaphore()
    peers = [sibling, far, near] + [along_x(d) for d in (1, 2, 3)] + [along_z(d) for d in range(1, 8)]
    for peer in peers:
        pl.semaphore_signal(barrier, inc=1, device_id=peer, device_id_type=pl.DeviceIdType.MESH)
    pl.semaphore_wait(barrier, len(peers))

    got, sib = {}, {}

    def rows_at(d, half, other, which=None):
        span = pl.ds(place(d, half) + other * rows, rows)
        return act.at[:, span] if which is None else act.at[which, span]

    def ring(j, half):
        for sign in (1, -1):
            which = None if j < 4 else (0 if sign == 1 else 1)
            src, dst = -sign * (j - 1), (-sign * j if j < 4 else 4)
            got[sign, j, half] = send(
                rows_at(src, half, 0, which), rows_at(dst, half, 0, which), along_z(sign)
            )
            sent_act.append(got[sign, j, half])

    def to_sibling(d, half, which=None):
        sent_act.append(send(rows_at(d, half, 0, which), rows_at(d, half, 1, which), sibling))
        return sent_act[-1]

    waited = []

    def arrive(copy):
        if not any(copy is other for other in waited):
            waited.append(copy)
            copy.wait_recv()

    def a0():
        for copy in own:
            copy.wait()
        sib["far"] = send(rows_at(0, 0, 0), rows_at(0, 1, 0), far)
        sent_act.append(sib["far"])
        ring(1, 0)
        sib[0, 0] = [to_sibling(0, 0)]

    def a1():
        arrive(sib["far"])
        ring(1, 1)
        sib[0, 1] = [to_sibling(0, 1)]

    def forward(j, half):
        for sign in (1, -1):
            arrive(got[sign, j, half])
        if j < 4:
            ring(j + 1, half)
            for d in (j, -j):
                sib[d, half] = [to_sibling(d, half)]
        else:
            sib[4, half] = [to_sibling(4, half, 0), to_sibling(4, half, 1)]

    def ready(k):
        lo, hi = OFFSETS[k], OFFSETS[k] + CHUNKS[k]
        for i, unit in enumerate(UNITS):
            if i * 2 * rows < hi and (i + 1) * 2 * rows > lo:
                for copy in sib[unit]:
                    arrive(copy)
        for copy in weights:
            if not any(copy is other for other in waited):
                waited.append(copy)
                copy.wait()

    def sizes(k):
        return OFFSETS[k], CHUNKS[k], CHUNKS[k] // 2, CHUNKS[k] // 8

    def start_sum(a, k, x_first, term):
        o, n, q, r = sizes(k)
        a.own[pl.ds(o, n)] = term
        if x_first:
            a.s1x[pl.ds(SAME[k], n)] = term.astype(BF16)
            a.first[k] = [
                send(
                    a.s1x.at[at(SAME[k] + y * q + x_of(d) * r, r)],
                    a.r1x.at[d - 1, y, pl.ds(SAME[k] // 8, r)],
                    along_x(d),
                )
                for d in (1, 3, 2) for y in (0, 1)
            ]
        else:
            half = pl.ds(SAME[k] // 2, q)
            a.s1y[half] = a.own[at(o + (1 - yl) * q, q)].astype(BF16)
            a.first[k] = [send(a.s1y.at[half], a.r1y.at[half], near)]

    def go_on(a, k, x_first):
        o, n, q, r = sizes(k)
        half, piece = pl.ds(SAME[k] // 2, q), pl.ds(SAME[k] // 8, r)
        for copy in a.first[k]:
            arrive(copy)
        if x_first:
            def total(y):
                value = a.own[at(o + y * q + x * r, r)]
                for d in range(3):
                    value = value + a.r1x[d, y, piece].astype(F32)
                return value

            a.s2y[piece] = total(1 - yl).astype(BF16)
            a.second[k] = [send(a.s2y.at[piece], a.r2y.at[piece], near)]
            a.fin[piece] = total(yl)
        else:
            a.s2x[half] = (a.own[at(o + yl * q, q)] + a.r1y[half].astype(F32)).astype(BF16)
            a.second[k] = [
                send(a.s2x.at[at(SAME[k] // 2 + x_of(d) * r, r)], a.r2x.at[d - 1, piece], along_x(d))
                for d in (1, 3, 2)
            ]

    def end_sum(a, k, x_first):
        o, n, q, r = sizes(k)
        piece = pl.ds(SAME[k] // 8, r)
        for copy in a.second[k]:
            arrive(copy)
        if x_first:
            return a.fin[piece] + a.r2y[piece].astype(F32)
        value = a.own[at(o + yl * q + x * r, r)] + a.r1y[at(SAME[k] // 2 + x * r, r)].astype(F32)
        for d in range(3):
            value = value + a.r2x[d, piece].astype(F32)
        return value

    def s1a(k):
        ready(k)
        start_sum(gu, k, X_FIRST[k], dot(act[0, pl.ds(OFFSETS[k], CHUNKS[k])], wgu[...], 1, 1))

    def s1b(k):
        ready(k)
        start_sum(h, k, not X_FIRST[k], dot(act[1, pl.ds(OFFSETS[k], CHUNKS[k])], dw[...], 1, 1))

    def s2a(k):
        go_on(h if X_FIRST[k] else gu, k, False)

    def s2b(k):
        go_on(gu if X_FIRST[k] else h, k, True)

    pa_y, pa_x, pb_y, pb_x, pa_xx, pb_yy = {}, {}, {}, {}, {}, {}

    def rows_of(k, y, of):
        o, n, q, r = sizes(k)
        return at(o + y * q + of * r, r)

    def same(ref, span, device):
        return send(ref.at[span], ref.at[span], device)

    def ways(k):
        return (1, 3) if FORWARD[k] else (1, 3, 2)

    def s3(k):
        g = end_sum(gu, k, X_FIRST[k])
        hidden_grad = end_sum(h, k, not X_FIRST[k])
        gate, up = g[:, :units], g[:, units:]
        sigmoid_gate = jax.nn.sigmoid(gate)
        span = rows_of(k, yl, x)
        up_part = hidden_grad * gate * sigmoid_gate
        gate_part = hidden_grad * up * sigmoid_gate * (1.0 + gate * (1.0 - sigmoid_gate))
        pa[span] = jnp.concatenate([gate_part, up_part], axis=1).astype(BF16)
        pa_y[k] = same(pa, span, near)
        pa_x[k] = {d: same(pa, span, along_x(d)) for d in ways(k)}
        pb[span] = (gate * sigmoid_gate * up).astype(BF16)

    def s3b(k):
        span = rows_of(k, yl, x)
        pb_x[k] = {d: same(pb, span, along_x(d)) for d in ways(k)}
        pb_y[k] = same(pb, span, near)

    def s4a(k):
        arrive(pa_y[k])
        span = rows_of(k, 1 - yl, x)
        pa_xx[k] = {d: same(pa, span, along_x(d)) for d in ways(k)}

    def s4f1(k):
        arrive(pa_x[k][1])
        pa_x[k][2] = same(pa, rows_of(k, yl, x_of(3)), along_x(1))

    def s4f2(k):
        arrive(pa_xx[k][3])
        pa_xx[k][2] = same(pa, rows_of(k, 1 - yl, x_of(1)), along_x(3))

    def s4b(k):
        pb_yy[k] = []
        for d in ways(k):
            arrive(pb_x[k][d])
            pb_yy[k].append(same(pb, rows_of(k, yl, x_of(4 - d)), near))
        if FORWARD[k]:
            d = 1 if k % 2 else 3
            pb_x[k][2] = same(pb, rows_of(k, yl, x_of(4 - d)), along_x(d))

    def s4c(k):
        arrive(pb_x[k][2])
        pb_yy[k].append(same(pb, rows_of(k, yl, x_of(2)), near))

    def s5(k):
        for copy in (*pa_x[k].values(), *pa_xx[k].values()):
            arrive(copy)
        span = pl.ds(OFFSETS[k], CHUNKS[k])
        ip[span] = dot(pa[span], wgu[...], 1, 0)

    summed = []

    def s6(g):
        for k in GROUPS[g]:
            for copy in [pb_y[k]] + pb_yy[k]:
                arrive(copy)
        span = pl.ds(OFFSETS[GROUPS[g][0]], sum(CHUNKS[k] for k in GROUPS[g]))
        gu_term = dot(pa[span], act[0, span], 0, 0)
        acc_gu[...] = acc_gu[...] + gu_term if summed else gu_term
        d_term = dot(pb[span], act[1, span], 0, 0)
        acc_d[...] = acc_d[...] + d_term if summed else d_term
        summed.append(g)

    dc, dy, dz = {}, {}, {}

    def d1(s, half):
        start = place(SLOTS[s], half)
        dc[s, half] = send(ip.at[pl.ds(start + rows, rows)], d_r1.at[s, half], sibling)

    def both(s, half):
        arrive(dc[s, half])
        return ip[pl.ds(place(SLOTS[s], half), rows)] + d_r1[s, half]

    def d2(s):
        value = both(s, 1)
        if s == 0:
            for i, d in enumerate(NEAR_Z):
                arrive(dz[SLOTS.index(d)])
                value = value + d_rz[i, 1].astype(F32)
        d_s2[s] = value.astype(BF16)
        dy[s] = send(d_s2.at[s], d_r2.at[s], far)

    def d3(s):
        if SLOTS[s] in NEAR_Z:
            i = NEAR_Z.index(SLOTS[s])
            for half in (0, 1):
                d_sz[i, half] = both(s, half).astype(BF16)
            dz[s] = send(d_sz.at[i], d_rz.at[i], along_z(SLOTS[s]))
        else:
            value = both(s, 0)
            arrive(dy[s])
            d_s3[s] = (value + d_r2[s].astype(F32)).astype(BF16)
            dz[s] = send(d_s3.at[s], d_r3.at[s - 1], along_z(SLOTS[s]))

    outs = []

    def d4():
        value = both(0, 0)
        arrive(dy[0])
        value = value + d_r2[0].astype(F32)
        for s in range(1, 8):
            arrive(dz[s])
            if SLOTS[s] in NEAR_Z:
                value = value + d_rz[NEAR_Z.index(SLOTS[s]), 0].astype(F32)
            else:
                value = value + d_r3[s - 1].astype(F32)
        ig_v[...] = value.astype(BF16)
        outs.append(local(ig_v, ig_out))

    def fin():
        for copy in sent_act:
            copy.wait_send()
        first, second = pl.ds(0, units), pl.ds(units, units)
        act[0, pl.ds(0, 2 * units)] = acc_gu[...].astype(BF16)
        outs.append(local(act.at[0, first], gg_out))
        outs.append(local(act.at[0, second], ug_out))
        act[1, first] = acc_d[...].astype(BF16)
        outs.append(local(act.at[1, first], dg_out))

    steps = {
        "A0": a0, "A1": a1, "R": forward, "s1a": s1a, "s1b": s1b, "s2a": s2a, "s2b": s2b, "s3": s3, "s3b": s3b,
        "s4a": s4a, "s4f1": s4f1, "s4f2": s4f2, "s4b": s4b, "s4c": s4c, "s5": s5, "s6": s6,
        "d1": d1, "d2": d2, "d3": d3, "d4": d4, "fin": fin,
    }
    for name, *where in ORDER:
        steps[name](*where)
    for copy in copies:
        if not any(copy is other for other in sent_act):
            copy.wait_send()
    for copy in outs:
        copy.wait()


def on_device(tokens, cotangent, gate_weight, up_weight, down_weight):
    rows, width = tokens.shape
    units = down_weight.shape[0]
    n = rows * 32
    scratch = [
        ((2, n, width), BF16), ((2 * units, width), BF16), ((units, width), BF16),
        *Sum.shapes(2 * units, X_ROWS, Y_ROWS), *Sum.shapes(units, Y_ROWS, X_ROWS),
        ((n, 2 * units), BF16), ((n, units), BF16), ((n, width), F32),
        ((8, 2, rows, width), F32), ((8, rows, width), BF16), ((8, rows, width), BF16),
        ((8, rows, width), BF16), ((7, rows, width), BF16),
        ((max(len(NEAR_Z), 1), 2, rows, width), BF16), ((max(len(NEAR_Z), 1), 2, rows, width), BF16),
        ((2 * units, width), F32), ((units, width), F32),
        ((rows, width), BF16),
    ]
    input_grad, gate_grad, up_grad, down_grad = pl.pallas_call(
        kernel,
        out_shape=[
            jax.ShapeDtypeStruct(a.shape, BF16) for a in (tokens, down_weight, down_weight, down_weight)
        ],
        in_specs=[pl.BlockSpec(memory_space=pl.ANY)] * 5,
        out_specs=[pl.BlockSpec(memory_space=pl.ANY)] * 4,
        scratch_shapes=[pltpu.VMEM(shape, dtype) for shape, dtype in scratch]
        + [
            pltpu.SemaphoreType.DMA((COPIES,)),
            pltpu.SemaphoreType.DMA((COPIES,)),
            pltpu.SemaphoreType.DMA((16,)),
        ],
        compiler_params=pltpu.CompilerParams(
            collective_id=0, has_side_effects=True, vmem_limit_bytes=61 * 2**20
        ),
        cost_estimate=pl.CostEstimate(
            flops=16 * n * width * units, bytes_accessed=6 * 2**20, transcendentals=n * units // 8
        ),
    )(tokens, cotangent, gate_weight.T, up_weight.T, down_weight)
    return input_grad, gate_grad.T, up_grad.T, down_grad


def solution(mesh):
    blocks = ("gx", "gy")
    by_row, by_column = P(blocks, "gz"), P("gz", blocks)
    return jax.shard_map(
        on_device,
        mesh=mesh,
        in_specs=(by_row, by_row, by_column, by_column, by_row),
        out_specs=(by_row, by_column, by_column, by_row),
        check_vma=False,
    )
```

time: 443 us -> 123 us (0.28)
  waiting for transfers between devices: 319 us -> 0 us
  Pallas kernels: 0 us -> 116 us
  blocking collectives: 55.3 us -> 0 us
  matrix products: 28.9 us -> 0 us
  between operations: 13.9 us -> 0.64 us
  starting transfers between devices: 10.1 us -> 0 us
  other arithmetic: 6.38 us -> 0 us
    all_gather x3 -> x0, waiting for transfers between devices: 255 us -> none  [the longest x1 91.5 us: on_device(): parts = lax.all_gather(parts, 'gz', axis=0, tiled=True)]
    pallas_call x0 -> x1, Pallas kernels: none -> 116 us  [on_device(): pl.pallas_call(kernel, out_shape=[jax.ShapeDtypeStruct(a.shape, BF16) for...]
    all_to_all x1 -> x0, waiting for transfers between devices: 62.7 us -> none  [summed(): landed = lax.all_to_all(sent, axes, split_axis=0, concat_axis=0)]
    all_to_all x1 -> x0, blocking collectives: 55.3 us -> none  [summed(): landed = lax.all_to_all(sent, axes, split_axis=0, concat_axis=0)]
    dot_general x8 -> x0, matrix products: 28.9 us -> none  [contract(): lax.dot_general(left, right, ((dims[:1], dims[1:]), ((), ())), preferred_...]
    all_to_all x1 -> x0, starting transfers between devices: 10 us -> none  [summed(): landed = lax.all_to_all(sent, axes, split_axis=0, concat_axis=0)]
    concatenate x2 -> x0, local copies, waits for them, and re-layouts: 7.54 us -> none  [the longest x1 6.5 us: on_device(): jnp.concatenate([contract(tokens_all, gate_weight, (1, 0)).astype(jnp.bfl...]
    unnamed x16 -> x8, local copies, waits for them, and re-layouts: 0.04 us -> 6.22 us
  transfers between devices with their start and end apart: 4 -> 0, of which waited for: 4 -> 0; matrix products, arithmetic and copies ran while one was open for 4% -> 0% of each run, Pallas kernels for 0% -> 0%
where the time goes in v3:
time: 123 us; the launch traced here: 122 us
  Pallas kernels  116 us (94%)
  local copies, waits for them, and re-layouts  6.22 us (5%)
    pallas_call x1, Pallas kernels, on_device(): pl.pallas_call(kernel, out_shape=[jax.ShapeDtypeStruct(a.shape, BF16) for...  116 us
    unnamed x8, local copies, waits for them, and re-layouts  6.22 us

profile of v3, /device:TPU:32, one launch (start us, length us, event | category | flops | bytes accessed | tf_op | source)
XLA Modules:
  0.0 122.5 jit_solution(17481247547511792483)
XLA Ops:
  0.6 115.6 %shard_map.84 = (bf16[48,1024]{1,0:T(8,128)(2,1)}, bf16[448,1024]{1,0:T(8,128)(2,1)}, bf16[448,1024]{1,0:T(8,128)(2,1)}, bf16[448,1024]{1,0:T(8,128)(2,1)}) custom-call(bf16[48,1024]{1,0:T(8,128)(2,1)} %tok_in.1, bf16[48,1024]{1,0:T(8,128)(2,1)} %cot_in.1, bf16[448,1024]{1,0:T(8,128)(2,1)} %bitcast.6, bf16[448,1024]{1,0:T(8,128)(2,1)} %bitcast.7, ...), custom_call_target="tpu_custom_call" | custom-call | flops 11274289152 | bytes 6291456 | tf_op jit(solution)/shard_map/pallas_call | solution.py:424
  116.3 1.5 %copy.13 = bf16[48,1024]{1,0:T(8,128)(2,1)} copy(bf16[48,1024]{1,0:T(8,128)(2,1)} %get-tuple-element.16) | data formatting | bytes 196608
  117.8 0.0 copy-start.1
  117.8 2.2 %copy.14 = bf16[1024,448]{0,1:T(8,128)(2,1)} copy(bf16[1024,448]{0,1:T(8,128)(2,1)} %bitcast.5) | data formatting | bytes 1835008
  120.1 0.0 copy-done.1
  120.1 0.0 copy-start
  120.1 0.9 copy.15
  121.0 0.6 copy-done
  121.6 0.9 copy.16
Async XLA Ops:
  117.8 2.2 %copy-start.1 = (bf16[448,1024]{1,0:T(8,128)(2,1)S(1)}, bf16[448,1024]{1,0:T(8,128)(2,1)}, u32[]{:S(2)}) copy-start(bf16[448,1024]{1,0:T(8,128)(2,1)} %get-tuple-element.10) | copy-start | bytes 2752516
  120.1 1.5 %copy-start = (bf16[448,1024]{1,0:T(8,128)(2,1)S(1)}, bf16[448,1024]{1,0:T(8,128)(2,1)}, u32[]{:S(2)}) copy-start(bf16[448,1024]{1,0:T(8,128)(2,1)} %get-tuple-element.19) | copy-start | bytes 2752516

commit v4 on v3

--- a/solution.py
+++ b/solution.py
@@ -30,13 +30,13 @@
     ("s4f1", 7), ("s4f2", 4), ("s4c", 3), ("s4c", 4), ("s3", 10), ("s3b", 10), ("s4a", 6), ("s5", 5),
     ("d1", 4, 0), ("s4a", 9), ("s4b", 6), ("s4c", 7), ("s4f2", 7), ("s3", 8), ("s3b", 8), ("s4b", 9),
     ("s4a", 10), ("s4f1", 6), ("s5", 3), ("d1", 1, 1), ("s6", 1), ("s4b", 10), ("s4f2", 6), ("d3", 1),
-    ("s4f1", 9), ("s3", 11), ("s4f2", 9), ("s4c", 6), ("s3b", 11), ("s4f1", 10), ("s5", 4), ("d1", 2, 1),
-    ("d1", 3, 0), ("s5", 7), ("s6", 2), ("s4b", 8), ("s4f2", 10), ("d3", 2), ("s4c", 9), ("s4f1", 8),
-    ("s4a", 8), ("s4c", 10), ("s5", 6), ("d1", 3, 1), ("d1", 4, 1), ("s6", 3), ("s4b", 11), ("s4f1", 11),
-    ("s4a", 11), ("s5", 9), ("d1", 5, 1), ("d3", 3), ("d3", 4), ("s4c", 8), ("s5", 10), ("d1", 6, 1), ("d2", 5),
-    ("s4f2", 8), ("d2", 6), ("s4f2", 11), ("s4c", 11), ("s5", 8), ("d1", 5, 0), ("d1", 6, 0), ("s6", 4),
-    ("s5", 11), ("d1", 7, 1), ("d1", 7, 0), ("d3", 5), ("s6", 5), ("d2", 7), ("d3", 6), ("fin",), ("d2", 0),
-    ("d3", 7), ("d4",),
+    ("s4f1", 9), ("s3", 11), ("s4f2", 9), ("s4c", 6), ("s4f1", 10), ("s3b", 11), ("s5", 4), ("d1", 2, 1),
+    ("d1", 3, 0), ("s6", 2), ("s4b", 8), ("s4a", 8), ("s5", 7), ("s4f2", 10), ("d3", 2), ("s4c", 9),
+    ("s4f1", 8), ("s4c", 10), ("s5", 6), ("d1", 3, 1), ("d1", 4, 1), ("s6", 3), ("s4b", 11), ("s4f1", 11),
+    ("s4a", 11), ("s5", 9), ("d1", 5, 1), ("d3", 3), ("d3", 4), ("s4c", 8), ("s4f2", 8), ("s5", 10),
+    ("d1", 6, 1), ("d2", 5), ("d2", 6), ("s4f2", 11), ("s4c", 11), ("s5", 8), ("d1", 5, 0), ("d1", 6, 0),
+    ("s6", 4), ("s5", 11), ("d1", 7, 1), ("d1", 7, 0), ("d3", 5), ("s6", 5), ("d2", 7), ("d3", 6), ("fin",),
+    ("d2", 0), ("d3", 7), ("d4",),
 )
 
 OFFSETS = tuple(sum(CHUNKS[:i]) for i in range(len(CHUNKS)))
@@ -77,7 +77,7 @@
     gu, h = Sum(scratch[3:13]), Sum(scratch[13:23])
     (
         pa, pb, ip, d_r1, d_s2, d_r2, d_s3, d_r3, d_sz, d_rz,
-        acc_gu, acc_d, ig_v, send_sem, recv_sem, local_sem,
+        acc_gu, acc_d, ig_v, wt, dt, send_sem, recv_sem, local_sem,
     ) = scratch[23:]
     rows, units = tok_in.shape[0], gw_in.shape[0]
     z, gy, gz = lax.axis_index("gx"), lax.axis_index("gy"), lax.axis_index("gz")
@@ -166,6 +166,10 @@
         sent_act.append(sib["far"])
         ring(1, 0)
         sib[0, 0] = [to_sibling(0, 0)]
+        for copy in weights:
+            copy.wait()
+        wt[...] = wgu[...].T
+        dt[...] = dw[...].T
 
     def a1():
         arrive(sib["far"])
@@ -188,10 +192,6 @@
             if i * 2 * rows < hi and (i + 1) * 2 * rows > lo:
                 for copy in sib[unit]:
                     arrive(copy)
-        for copy in weights:
-            if not any(copy is other for other in waited):
-                waited.append(copy)
-                copy.wait()
 
     def sizes(k):
         return OFFSETS[k], CHUNKS[k], CHUNKS[k] // 2, CHUNKS[k] // 8
@@ -250,11 +250,11 @@
 
     def s1a(k):
         ready(k)
-        start_sum(gu, k, X_FIRST[k], dot(act[0, pl.ds(OFFSETS[k], CHUNKS[k])], wgu[...], 1, 1))
+        start_sum(gu, k, X_FIRST[k], dot(act[0, pl.ds(OFFSETS[k], CHUNKS[k])], wt[...], 1, 0))
 
     def s1b(k):
         ready(k)
-        start_sum(h, k, not X_FIRST[k], dot(act[1, pl.ds(OFFSETS[k], CHUNKS[k])], dw[...], 1, 1))
+        start_sum(h, k, not X_FIRST[k], dot(act[1, pl.ds(OFFSETS[k], CHUNKS[k])], dt[...], 1, 0))
 
     def s2a(k):
         go_on(h if X_FIRST[k] else gu, k, False)
@@ -407,6 +407,12 @@
         copy.wait()
 
 
+def hand_over(*refs):
+    n = len(refs) // 2
+    for i in range(n):
+        refs[n + i][...] = refs[i][...]
+
+
 def on_device(tokens, cotangent, gate_weight, up_weight, down_weight):
     rows, width = tokens.shape
     units = down_weight.shape[0]
@@ -419,13 +425,14 @@
         ((8, rows, width), BF16), ((7, rows, width), BF16),
         ((max(len(NEAR_Z), 1), 2, rows, width), BF16), ((max(len(NEAR_Z), 1), 2, rows, width), BF16),
         ((2 * units, width), F32), ((units, width), F32),
-        ((rows, width), BF16),
+        ((rows, width), BF16), ((width, 2 * units), BF16), ((width, units), BF16),
     ]
-    input_grad, gate_grad, up_grad, down_grad = pl.pallas_call(
+    results = [
+        jax.ShapeDtypeStruct(a.shape, BF16) for a in (tokens, down_weight, down_weight, down_weight)
+    ]
+    values = pl.pallas_call(
         kernel,
-        out_shape=[
-            jax.ShapeDtypeStruct(a.shape, BF16) for a in (tokens, down_weight, down_weight, down_weight)
-        ],
+        out_shape=results,
         in_specs=[pl.BlockSpec(memory_space=pl.ANY)] * 5,
         out_specs=[pl.BlockSpec(memory_space=pl.ANY)] * 4,
         scratch_shapes=[pltpu.VMEM(shape, dtype) for shape, dtype in scratch]
@@ -441,6 +448,10 @@
             flops=16 * n * width * units, bytes_accessed=6 * 2**20, transcendentals=n * units // 8
         ),
     )(tokens, cotangent, gate_weight.T, up_weight.T, down_weight)
+    input_grad, gate_grad, up_grad, down_grad = pl.pallas_call(
+        hand_over,
+        out_shape=results,
+    )(*values)
     return input_grad, gate_grad.T, up_grad.T, down_grad
 
 

time: 123 us -> 119 us (0.967)
  local copies, waits for them, and re-layouts: 6.22 us -> 0 us
    unnamed x8 -> x0, local copies, waits for them, and re-layouts: 6.22 us -> none
    pallas_call x1 -> x2, Pallas kernels: 116 us -> 117 us  [the longest x1 114 us: on_device(): pl.pallas_call(kernel, out_shape=results, in_specs=[pl.BlockSpec(memory_s...]
where the time goes in v4:
time: 119 us; the launch traced here: 118 us
  Pallas kernels  117 us (98%)
    pallas_call x1, Pallas kernels, on_device(): pl.pallas_call(kernel, out_shape=results, in_specs=[pl.BlockSpec(memory_s...  114 us
    pallas_call x1, Pallas kernels, on_device(): pl.pallas_call(hand_over, out_shape=results)(*values)  3.38 us

profile of v4, /device:TPU:32, one launch (start us, length us, event | category | flops | bytes accessed | tf_op | source)
XLA Modules:
  0.0 117.7 jit_solution(17805077168588693767)
XLA Ops:
  0.6 113.6 %shard_map.84 = (bf16[48,1024]{1,0:T(8,128)(2,1)}, bf16[448,1024]{1,0:T(8,128)(2,1)}, bf16[448,1024]{1,0:T(8,128)(2,1)}, bf16[448,1024]{1,0:T(8,128)(2,1)}) custom-call(bf16[48,1024]{1,0:T(8,128)(2,1)} %tok_in.1, bf16[48,1024]{1,0:T(8,128)(2,1)} %cot_in.1, bf16[448,1024]{1,0:T(8,128)(2,1)} %bitcast.4, bf16[448,1024]{1,0:T(8,128)(2,1)} %bitcast.5, ...), custom_call_target="tpu_custom_call" | custom-call | flops 11274289152 | bytes 6291456 | tf_op jit(solution)/shard_map/pallas_call | solution.py:433
  114.3 3.4 %shard_map.85 = (bf16[48,1024]{1,0:T(8,128)(2,1)}, bf16[448,1024]{1,0:T(8,128)(2,1)}, bf16[448,1024]{1,0:T(8,128)(2,1)}, bf16[448,1024]{1,0:T(8,128)(2,1)}) custom-call(bf16[48,1024]{1,0:T(8,128)(2,1)} %get-tuple-element.12.refs_0_, bf16[448,1024]{1,0:T(8,128)(2,1)} %get-tuple-element.13.refs_1_, bf16[448,1024]{1,0:T(8,128)(2,1)} %get-tuple-element.14.refs_2_, ...), custom_call_target="tpu_custom_call" | custom-call | tf_op jit(solution)/shard_map/pallas_call | solution.py:451

commit v5 on v4

--- a/solution.py
+++ b/solution.py
@@ -67,7 +67,7 @@
             ((x_rows + y_rows, columns), F32),
             ((y // 2, columns), BF16), ((y // 2, columns), BF16),
             ((y // 2, columns), BF16), ((3, y // 8, columns), BF16),
-            ((x, columns), BF16), ((3, 2, x // 8, columns), BF16),
+            ((2, x // 2, columns), BF16), ((3, 2, x // 8, columns), BF16),
             ((x // 8, columns), BF16), ((x // 8, columns), BF16), ((x // 8, columns), F32),
         ]
 
@@ -200,14 +200,14 @@
         o, n, q, r = sizes(k)
         a.own[pl.ds(o, n)] = term
         if x_first:
-            a.s1x[pl.ds(SAME[k], n)] = term.astype(BF16)
+            a.s1x[:, pl.ds(SAME[k] // 2, q)] = term.astype(BF16).reshape(2, q, -1)
             a.first[k] = [
                 send(
-                    a.s1x.at[at(SAME[k] + y * q + x_of(d) * r, r)],
-                    a.r1x.at[d - 1, y, pl.ds(SAME[k] // 8, r)],
+                    a.s1x.at[:, at(SAME[k] // 2 + x_of(d) * r, r)],
+                    a.r1x.at[d - 1, :, pl.ds(SAME[k] // 8, r)],
                     along_x(d),
                 )
-                for d in (1, 3, 2) for y in (0, 1)
+                for d in (1, 3, 2)
             ]
         else:
             half = pl.ds(SAME[k] // 2, q)

time: 119 us -> 119 us (level)
  no operation moved by 1% of the time
where the time goes in v5:
time: 119 us; the launch traced here: 118 us
  Pallas kernels  117 us (98%)
    pallas_call x1, Pallas kernels, on_device(): pl.pallas_call(kernel, out_shape=results, in_specs=[pl.BlockSpec(memory_s...  114 us
    pallas_call x1, Pallas kernels, on_device(): pl.pallas_call(hand_over, out_shape=results)(*values)  3.38 us

profile of v5, /device:TPU:32, one launch (start us, length us, event | category | flops | bytes accessed | tf_op | source)
XLA Modules:
  0.0 117.7 jit_solution(4897323852993192316)
XLA Ops:
  0.6 113.7 %shard_map.84 = (bf16[48,1024]{1,0:T(8,128)(2,1)}, bf16[448,1024]{1,0:T(8,128)(2,1)}, bf16[448,1024]{1,0:T(8,128)(2,1)}, bf16[448,1024]{1,0:T(8,128)(2,1)}) custom-call(bf16[48,1024]{1,0:T(8,128)(2,1)} %tok_in.1, bf16[48,1024]{1,0:T(8,128)(2,1)} %cot_in.1, bf16[448,1024]{1,0:T(8,128)(2,1)} %bitcast.4, bf16[448,1024]{1,0:T(8,128)(2,1)} %bitcast.5, ...), custom_call_target="tpu_custom_call" | custom-call | flops 11274289152 | bytes 6291456 | tf_op jit(solution)/shard_map/pallas_call | solution.py:433
  114.3 3.4 %shard_map.85 = (bf16[48,1024]{1,0:T(8,128)(2,1)}, bf16[448,1024]{1,0:T(8,128)(2,1)}, bf16[448,1024]{1,0:T(8,128)(2,1)}, bf16[448,1024]{1,0:T(8,128)(2,1)}) custom-call(bf16[48,1024]{1,0:T(8,128)(2,1)} %get-tuple-element.12.refs_0_, bf16[448,1024]{1,0:T(8,128)(2,1)} %get-tuple-element.13.refs_1_, bf16[448,1024]{1,0:T(8,128)(2,1)} %get-tuple-element.14.refs_2_, ...), custom_call_target="tpu_custom_call" | custom-call | tf_op jit(solution)/shard_map/pallas_call | solution.py:451
